TPU v7x, 256 devices: a whole 4x4x8 slice. The times are simulated.
256 devices in a mesh: grid: 4 (over x), slab: 64 (over y, z, core).
Axes of the slice: x: 4, y: 4, z: 8, core: 2. Of those that a mesh axis runs over, the one named last changes fastest.
Arguments:
- state: float32 [4, 5, 256, 256, 128], P('grid', None, 'slab'), may hold values from -2 to 5, as said below
- jacobian: float32 [4, 256, 256, 128], P('grid', 'slab'), may hold values from 0.5 to 2
- iblank: int32 [4, 256, 256, 1], P('grid', 'slab'), may hold values from 0 to 2
- donor_blocks: int32 [4, 4096, 2], P('grid', 'slab'), may hold values from 0 to 1023
- recv_blocks: int32 [4, 4096, 2], P('grid', 'slab'), may hold values from 0 to 1023, as said below
- deriv_a: float32 [4, 256, 256], P('grid')
- deriv_b: float32 [4, 256, 256], P('grid')
- filter_a: float32 [4, 256, 256], P('grid')
- filter_b: float32 [4, 256, 256], P('grid')
Outputs:
- advanced: float32 [4, 5, 256, 256, 128], P('grid', None, 'slab')
Inputs may be any that keep to these rules, and one draw needn't show every extreme that they name: `state`: state variable 0 (density) lies in 0.5 to 2, variable 4 (energy) in 2 to 5, momenta in -2 to 2. `recv_blocks`: within the rows of one slab position the entries are distinct; no block flagged 0 is among them, and every block flagged 2 is.
All inputs are finite; a program needn't handle non-finite values.
Results may differ from a plain program's by a relative error of at most 0.0003.
Values sent between devices are 32-bit elements; how exact they have to be, the bound alone decides.
No kernel may reach another device: no remote copies, remote signals or barrier semaphores. Data moves between devices by JAX's collectives and lax.ppermute only.
A program may use at most 64 MiB of HBM per device.

v0:
```python
import jax
import jax.numpy as jnp
from jax import lax
from jax.experimental import pallas as pl
from jax.experimental.pallas import tpu as pltpu
from jax.sharding import Mesh
from jax.sharding import PartitionSpec as P

V = 5
R = 4
N = 64
B = 256
L = 128
T = 2 * R
C = (V + 1) * T
Q = V * T
SLOTS = 128
EXTRA = Q
FREE = (1.0, 0.5, 0.0, 0.0, 2.5)

section_weight = 0.3
f32, bf16, i32 = jnp.float32, jnp.bfloat16, jnp.int32
VMEM = pl.BlockSpec(memory_space=pltpu.VMEM)
SMEM = pl.BlockSpec(memory_space=pltpu.SMEM)
HBM = pl.BlockSpec(memory_space=pltpu.HBM)


def params(mib):
    return pltpu.CompilerParams(vmem_limit_bytes=mib * 2**20)


def cost(nbytes, flops=0):
    return pl.CostEstimate(flops=flops, bytes_accessed=nbytes, transcendentals=0)


def pack_kernel(donors, targets, flags, holes, state, jacobian, sent, donor, target, flag, hole, u, jac, rows, out, sems):
    pairs = [(donors, donor), (targets, target), (flags, flag), (holes, hole), (jacobian, jac)]
    pairs += [(state.at[pl.ds(v * R * B, R * B)], u.at[pl.ds(v * R * B, R * B)]) for v in range(V)]
    fetch = [pltpu.make_async_copy(a, b, sems.at[i]) for i, (a, b) in enumerate(pairs)]
    for copy in fetch[3:] + fetch[:3]:
        copy.start()
    fetch[3].wait()
    lines_out = out.reshape(L, C, L)

    def send(v):
        at = pl.ds(v * T, T)
        copy = pltpu.make_async_copy(lines_out.at[:, at, :], sent.at[:, at, :], sems.at[V + 5 + v])
        copy.start()
        return copy

    sends = []
    for v in range(V):
        fetch[5 + v].wait()
        for r in range(R):
            for h in range(2):
                turned = u[(v * R + r) * B + h * L : (v * R + r) * B + (h + 1) * L, :].T
                out[pl.ds(v * T + h * R + r, L, stride=C), :] = jnp.where(
                    hole[2 * r + h : 2 * r + h + 1, :] == 0, FREE[v], turned
                )
        sends.append(send(v))
    for i in (0, 1, 2, 4):
        fetch[i].wait()
    lanes = lax.broadcasted_iota(i32, (1, SLOTS), 1)

    def body(s, row):
        for kk in range(2):
            k = kk * N + s
            t = donor[kk, s]
            rows[pl.ds(k, V, stride=SLOTS), :] = u[pl.ds(t, V, stride=R * B), :]
            rows[pl.ds(V * SLOTS + k, 1), :] = jac[pl.ds(t, 1), :]
            t = target[kk, s]
            rows[pl.ds((V + 1) * SLOTS + k, 1), :] = jac[pl.ds(t, 1), :]
            row = jnp.where(lanes == k, jnp.where(flag[t] == 2, t, -1), row)
        return row

    row = lax.fori_loop(0, N, body, jnp.full((1, SLOTS), -1, i32), unroll=8)
    for e in range(V + 2):
        out[pl.ds(EXTRA + e, L, stride=C), :] = rows[e * SLOTS : (e + 1) * SLOTS, :].T
    out[pl.ds(EXTRA + V + 2, L, stride=C), :] = jnp.broadcast_to(row.astype(f32), (L, SLOTS))
    sends.append(send(V))
    for copy in sends:
        copy.wait()


def matrix_kernel(da, db, fa, fb, out, rows):
    for at, matrix in ((0, da), (2, fa)):
        turned = matrix[...]
        for _ in range(2):
            for h in range(2):
                rows[h] = turned[:, h * L : (h + 1) * L]
            sorted_rows = [
                jnp.concatenate([rows[h, pl.ds(r, N, stride=R), :] for h in range(2)], axis=1) for r in range(R)
            ]
            turned = jnp.concatenate(sorted_rows, axis=0).T
        out[at] = turned
    out[1] = db[...].T
    out[3] = fb[...].T


def split(value):
    high = value.astype(bf16)
    return high, (value - high.astype(f32)).astype(bf16)


def dot(a, b):
    return jnp.dot(a, b, preferred_element_type=f32)


def plane_kernel(half, recv, mine, theirs, out, prep, left, column, field, ah, al, bh, bl, here, sems):
    fetch = [pltpu.make_async_copy(mine, here.at[0], sems.at[0]), pltpu.make_async_copy(theirs, here.at[1], sems.at[1])]
    for copy in fetch:
        copy.start()

    for g in range(2):
        def rows(grid, e):
            return recv[pl.ds(grid * N * C + EXTRA + e, N, stride=C), :]

        def swapped(e):
            turned = rows(1 - g, e).T
            return jnp.concatenate([turned[:N], turned[N:]], axis=1)

        weight = swapped(V)
        weight = weight / (weight + rows(g, V + 1))
        target = rows(g, V + 2).astype(i32)
        column[g * N : (g + 1) * N] = target & (L - 1)
        target = target >> 7
        for v in range(V + 1):
            value = weight if v == V else weight * swapped(v)
            for h in range(2):
                for r in range(R):
                    left[pl.ds(g * N * C + v * T + h * R + r, N, stride=C), :] = jnp.where(
                        target == 2 * r + h, value, 0.0
                    )

    places = lax.broadcasted_iota(i32, (L, SLOTS), 0)

    def scatter(s, carry):
        at = pl.multiple_of(s * C, 8)
        high, low = split(left[pl.ds(at, C), :])
        hit = (places == column[pl.ds(s, 1), :]).astype(f32).astype(bf16)
        spread = lax.dot_general(
            jnp.concatenate([high, low], axis=0), hit, (((1,), (1,)), ((), ())), preferred_element_type=f32
        )
        spread = spread[:C] + spread[C:]
        keep = 1.0 - spread[Q:]
        for v in range(V):
            prep[pl.ds(at + v * T, T), :] = spread[v * T : (v + 1) * T] + keep * recv[pl.ds(at + v * T, T), :]
        return carry

    lax.fori_loop(0, 2 * N, scatter, 0, unroll=64)
    for copy in fetch:
        copy.wait()

    for own in range(2):
        grid = jnp.bitwise_xor(half[0], own)
        da_h, da_l = split(here[own, 0])
        db_h, db_l = split(here[own, 1])
        fa_h, fa_l = split(here[own, 2])
        fb_h, fb_l = split(here[own, 3])
        for r in range(R):
            for h in range(2):
                u = [prep[pl.ds(grid * (N * C) + v * T + h * R + r, N, stride=C), :] for v in range(V)]
                cols = slice(h * L, (h + 1) * L)
                inverse = 1.0 / u[0]
                va, vb = u[1] * inverse, u[2] * inverse
                pressure = 0.4 * (u[4] - 0.5 * (u[1] * u[1] + u[2] * u[2] + u[3] * u[3]) * inverse)
                total = u[4] + pressure
                flux_a = [u[1], u[1] * va + pressure, u[2] * va, u[3] * va, total * va]
                flux_b = [u[2], u[1] * vb, u[2] * vb + pressure, u[3] * vb, total * vb]
                for v in range(V):
                    at = slice(v * B + r * N, v * B + (r + 1) * N)
                    field[at, cols] = u[v]
                    ah[at, cols], al[at, cols] = split(flux_a[v])
                    bh[at, cols], bl[at, cols] = split(flux_b[v])

        planes_at = [slice(v * B, (v + 1) * B) for v in range(V)]
        for at in planes_at:
            slope = dot(da_h, ah[at]) + dot(da_h, al[at]) + dot(da_l, ah[at])
            slope += dot(bh[at], db_h) + dot(bl[at], db_h) + dot(bh[at], db_l)
            ah[at], al[at] = split(field[at] - section_weight * slope)
        for at in planes_at:
            smooth = dot(ah[at], fb_h) + dot(al[at], fb_h) + dot(ah[at], fb_l)
            bh[at], bl[at] = split(smooth)
        for v, at in enumerate(planes_at):
            smooth = dot(fa_h, bh[at]) + dot(fa_h, bl[at]) + dot(fa_l, bh[at])
            for r in range(R):
                for h in range(2):
                    out[pl.ds(grid * (N * Q) + v * T + h * R + r, N, stride=Q), :] = smooth[
                        r * N : (r + 1) * N, h * L : (h + 1) * L
                    ]


def unpack_kernel(lines, result, out, sems):
    copies = []
    for v in range(V):
        for r in range(R):
            for h in range(2):
                out[v, r, h * L : (h + 1) * L, :] = lines[pl.ds(v * T + h * R + r, L, stride=Q), :].T
        copies.append(pltpu.make_async_copy(out.at[v], result.at[v], sems.at[v]))
        copies[-1].start()
    for copy in copies:
        copy.wait()


def pack(donors, targets, flags, state, jacobian):
    return pl.pallas_call(
        pack_kernel,
        out_shape=jax.ShapeDtypeStruct((L, C, L), f32),
        in_specs=[HBM] * 6,
        out_specs=HBM,
        scratch_shapes=[
            pltpu.SMEM((2, N), i32),
            pltpu.SMEM((2, N), i32),
            pltpu.SMEM((R * B,), i32),
            pltpu.VMEM((T, L), i32),
            pltpu.VMEM((V * R * B, L), f32),
            pltpu.VMEM((R * B, L), f32),
            pltpu.VMEM(((V + 2) * SLOTS, L), f32),
            pltpu.VMEM((L * C, L), f32),
            pltpu.SemaphoreType.DMA((2 * V + 6,)),
        ],
        compiler_params=params(58),
        cost_estimate=cost(8_000_000),
        name="pack",
    )(
        donors.T,
        targets.T,
        flags.reshape(R * B),
        flags.reshape(T, L),
        state.reshape(V * R * B, L),
        jacobian.reshape(R * B, L),
    )


def matrices(*given):
    return pl.pallas_call(
        matrix_kernel,
        out_shape=jax.ShapeDtypeStruct((4, B, B), f32),
        in_specs=[VMEM] * 4,
        out_specs=VMEM,
        scratch_shapes=[pltpu.VMEM((2, B, L), f32)],
        compiler_params=params(8),
        cost_estimate=cost(2_000_000),
        name="matrices",
    )(*given)


def planes(half, recv, mine, theirs):
    return pl.pallas_call(
        plane_kernel,
        out_shape=jax.ShapeDtypeStruct((L * Q, L), f32),
        in_specs=[SMEM, VMEM, HBM, HBM],
        out_specs=VMEM,
        scratch_shapes=[
            pltpu.VMEM((L * C, L), f32),
            pltpu.VMEM((L * C, SLOTS), f32),
            pltpu.VMEM((L, SLOTS), i32),
            pltpu.VMEM((V * B, B), f32),
        ]
        + [pltpu.VMEM((V * B, B), bf16)] * 4
        + [pltpu.VMEM((2, 4, B, B), f32), pltpu.SemaphoreType.DMA((2,))],
        compiler_params=params(40),
        cost_estimate=cost(8_000_000, 8_000_000_000),
        name="planes",
    )(half, recv, mine, theirs)


def unpack(lines):
    return pl.pallas_call(
        unpack_kernel,
        out_shape=jax.ShapeDtypeStruct((V, R, B, L), f32),
        in_specs=[VMEM],
        out_specs=HBM,
        scratch_shapes=[pltpu.VMEM((V, R, B, L), f32), pltpu.SemaphoreType.DMA((V,))],
        compiler_params=params(24),
        cost_estimate=cost(6_000_000),
        name="unpack",
    )(lines)


def exchange(value):
    return lax.all_to_all(value, ("half", "slab"), split_axis=0, concat_axis=0, tiled=True)


def local(state, jacobian, iblank, donor_blocks, recv_blocks, deriv_a, deriv_b, filter_a, filter_b):
    packed = pack(donor_blocks[0], recv_blocks[0], iblank[0], state[0], jacobian[0])
    recv = exchange(packed).reshape(L * C, L)
    mine = matrices(deriv_a[0], deriv_b[0], filter_a[0], filter_b[0])
    theirs = lax.ppermute(mine, "half", [(0, 1), (1, 0)])
    half = lax.axis_index("half").astype(i32)[None]
    lines = planes(half, recv, mine, theirs)
    result = exchange(lines.reshape(L, Q, L)).reshape(L * Q, L)
    return unpack(result)[None]


def solution(mesh):
    pairs = Mesh(mesh.devices.reshape(-1, 2, N), ("pair", "half", "slab"))
    grid = ("pair", "half")
    placed = (
        P(grid, None, "slab", None, None),
        P(grid, "slab", None, None),
        P(grid, "slab", None, None),
        P(grid, "slab", None),
        P(grid, "slab", None),
        P(grid, None, None),
        P(grid, None, None),
        P(grid, None, None),
        P(grid, None, None),
    )
    return jax.shard_map(
        local,
        mesh=pairs,
        in_specs=placed,
        out_specs=P(grid, None, "slab", None, None),
        check_vma=False,
    )
```

profile of v0, /device:TPU:1, one launch (start us, length us, event | category | flops | bytes accessed | tf_op | source)
XLA Modules:
  0.0 174.5 jit_solution(419595488913481575)
XLA Ops:
  0.0 4.4 %pack.1 = f32[128,48,128]{2,1,0:T(8,128)} custom-call(s32[2,64]{1,0:T(2,128)} %bitcast.30, s32[2,64]{1,0:T(2,128)} %bitcast.31, s32[1024]{0:T(1024)} %bitcast.28, s32[8,128]{1,0:T(8,128)} %bitcast.29, f32[5120,128]{1,0:T(8,128)} %bitcast.26, f32[1024,128]{1,0:T(8,128)} %bitcast.27), custom_call_target="tpu_custom_call" | custom-call | bytes 8000000 | tf_op jit(solution)/shard_map/pack/pallas_call | solution.py:206
  4.4 0.0 copy-start
  4.4 15.0 %all-to-all-start = ((f32[128,48,128]{2,1,0:T(8,128)}), f32[128,48,128]{2,1,0:T(8,128)S(1)}, u32[]{:S(2)}, u32[]{:S(2)}) async-start(f32[128,48,128]{2,1,0:T(8,128)} %pack.1), calls=%async_computation | async-start | bytes 6291456 | tf_op jit(solution)/shard_map/all_to_all | solution.py:282
  19.4 0.0 copy-done
  19.5 0.0 copy-start.1
  19.5 0.9 copy-done.1
  20.4 0.0 copy-start.2
  20.4 0.9 copy-done.2
  21.4 0.0 copy-start.3
  21.4 0.9 copy-done.3
  22.3 1.6 matrices.1.mine
  23.9 1.7 collective-permute-start
  25.6 42.8 %collective-permute-done.theirs = f32[4,256,256]{2,1,0:T(8,128)} collective-permute-done((f32[4,256,256]{2,1,0:T(8,128)}, f32[4,256,256]{2,1,0:T(8,128)}, u32[]{:S(2)}, u32[]{:S(2)}) %collective-permute-start) | collective-permute-done | bytes 1048608 | tf_op jit(solution)/shard_map/ppermute | solution.py:289
  68.4 24.3 %all-to-all-done = f32[128,48,128]{2,1,0:T(8,128)S(1)} async-done(((f32[128,48,128]{2,1,0:T(8,128)}), f32[128,48,128]{2,1,0:T(8,128)S(1)}, u32[]{:S(2)}, u32[]{:S(2)}) %all-to-all-start) | async-done | bytes 3145760 | tf_op jit(solution)/shard_map/all_to_all | solution.py:282
  92.7 9.9 %planes.1 = f32[5120,128]{1,0:T(8,128)S(1)} custom-call(s32[1]{0:T(128)} %bitcast.half, f32[6144,128]{1,0:T(8,128)S(1)} %bitcast.20, f32[4,256,256]{2,1,0:T(8,128)} %matrices.1.mine, f32[4,256,256]{2,1,0:T(8,128)} %collective-permute-done.theirs), custom_call_target="tpu_custom_call" | custom-call | flops 8000000000 | bytes 8000000 | tf_op jit(solution)/shard_map/planes/pallas_call | solution.py:249
  102.6 70.0 %all_to_all.10 = f32[128,40,128]{2,1,0:T(8,128)S(1)} all-to-all(f32[128,40,128]{2,1,0:T(8,128)S(1)} %bitcast.21), channel_id=1, replica_groups=mesh['pair'=2,'half'=2,'slab'=64] {'half','slab'}, dimensions={0} | all-to-all | bytes 5242880 | tf_op jit(solution)/shard_map/all_to_all | solution.py:282
  172.6 1.7 unpack.1
Async XLA Ops:
  4.4 15.0 %copy-start = (f32[1,256,256]{2,1,0:T(8,128)S(1)}, f32[1,256,256]{2,1,0:T(8,128)}, u32[]{:S(2)}) copy-start(f32[1,256,256]{2,1,0:T(8,128)} %param.14) | copy-start | bytes 786436
  4.4 88.2 %all-to-all-start = ((f32[128,48,128]{2,1,0:T(8,128)}), f32[128,48,128]{2,1,0:T(8,128)S(1)}, u32[]{:S(2)}, u32[]{:S(2)}) async-start(f32[128,48,128]{2,1,0:T(8,128)} %pack.1), calls=%async_computation | async-start | bytes 6291456 | tf_op jit(solution)/shard_map/all_to_all | solution.py:282
  19.5 1.0 copy-start.1
  20.4 0.9 copy-start.2
  21.4 0.9 copy-start.3
  23.9 44.5 %collective-permute-start = (f32[4,256,256]{2,1,0:T(8,128)}, f32[4,256,256]{2,1,0:T(8,128)}, u32[]{:S(2)}, u32[]{:S(2)}) collective-permute-start(f32[4,256,256]{2,1,0:T(8,128)} %matrices.1.mine), channel_id=1, source_target_pairs={{0,64},{64,0},{1,65},{65,1},{2,66},{66,2},{3,67},{67,3},{4,68},{68... | collective-permute-start | bytes 3145736 | tf_op jit(solution)/shard_map/ppermute | solution.py:289
where the time goes:
time: 175 us; the launch traced here: 174 us
  blocking collectives  70 us (40%)
  waiting for transfers between devices  67.1 us (38%)
  Pallas kernels  17.6 us (10%)
  starting transfers between devices  16.7 us (10%)
  local copies, waits for them, and re-layouts  2.85 us (2%)
    all_to_all x1, blocking collectives, exchange(): lax.all_to_all(value, ('half', 'slab'), split_axis=0, concat_axis=0, tile...  70 us
    ppermute x1, waiting for transfers between devices, local(): theirs = lax.ppermute(mine, 'half', [(0, 1), (1, 0)])  42.8 us
    all_to_all x1, waiting for transfers between devices, exchange(): lax.all_to_all(value, ('half', 'slab'), split_axis=0, concat_axis=0, tile...  24.3 us
    all_to_all x1, starting transfers between devices, exchange(): lax.all_to_all(value, ('half', 'slab'), split_axis=0, concat_axis=0, tile...  15 us
    pallas_call x1, Pallas kernels, planes(): pl.pallas_call(plane_kernel, out_shape=jax.ShapeDtypeStruct((L * Q, L), f...  9.88 us
    pallas_call x1, Pallas kernels, pack(): pl.pallas_call(pack_kernel, out_shape=jax.ShapeDtypeStruct((L, C, L), f32...  4.41 us
  transfers between devices with their start and end apart: 2, of which 2 were waited for; matrix products, arithmetic and copies ran while one was open for 0% of the time, Pallas kernels for 1%

commit v1 on v0

--- a/solution.py
+++ b/solution.py
@@ -15,6 +15,7 @@
 C = (V + 1) * T
 Q = V * T
 SLOTS = 128
+NOWHERE = 4 * R * B
 EXTRA = Q
 FREE = (1.0, 0.5, 0.0, 0.0, 2.5)
 
@@ -37,7 +38,7 @@
     pairs = [(donors, donor), (targets, target), (flags, flag), (holes, hole), (jacobian, jac)]
     pairs += [(state.at[pl.ds(v * R * B, R * B)], u.at[pl.ds(v * R * B, R * B)]) for v in range(V)]
     fetch = [pltpu.make_async_copy(a, b, sems.at[i]) for i, (a, b) in enumerate(pairs)]
-    for copy in fetch[3:] + fetch[:3]:
+    for copy in [fetch[3]] + fetch[5:] + [fetch[4]] + fetch[:3]:
         copy.start()
     fetch[3].wait()
     lines_out = out.reshape(L, C, L)
@@ -70,10 +71,10 @@
             rows[pl.ds(V * SLOTS + k, 1), :] = jac[pl.ds(t, 1), :]
             t = target[kk, s]
             rows[pl.ds((V + 1) * SLOTS + k, 1), :] = jac[pl.ds(t, 1), :]
-            row = jnp.where(lanes == k, jnp.where(flag[t] == 2, t, -1), row)
+            row = jnp.where(lanes == k, jnp.where(flag[t] == 2, t, NOWHERE), row)
         return row
 
-    row = lax.fori_loop(0, N, body, jnp.full((1, SLOTS), -1, i32), unroll=8)
+    row = lax.fori_loop(0, N, body, jnp.full((1, SLOTS), NOWHERE, i32), unroll=8)
     for e in range(V + 2):
         out[pl.ds(EXTRA + e, L, stride=C), :] = rows[e * SLOTS : (e + 1) * SLOTS, :].T
     out[pl.ds(EXTRA + V + 2, L, stride=C), :] = jnp.broadcast_to(row.astype(f32), (L, SLOTS))
@@ -106,7 +107,7 @@
     return jnp.dot(a, b, preferred_element_type=f32)
 
 
-def plane_kernel(half, recv, mine, theirs, out, prep, left, column, field, ah, al, bh, bl, here, sems):
+def plane_kernel(half, recv, mine, theirs, out, prep, high, low, place, field, ah, al, bh, bl, here, sems):
     fetch = [pltpu.make_async_copy(mine, here.at[0], sems.at[0]), pltpu.make_async_copy(theirs, here.at[1], sems.at[1])]
     for copy in fetch:
         copy.start()
@@ -119,35 +120,42 @@
             turned = rows(1 - g, e).T
             return jnp.concatenate([turned[:N], turned[N:]], axis=1)
 
+        at = slice(g * N, (g + 1) * N)
         weight = swapped(V)
         weight = weight / (weight + rows(g, V + 1))
-        target = rows(g, V + 2).astype(i32)
-        column[g * N : (g + 1) * N] = target & (L - 1)
-        target = target >> 7
+        place[at] = rows(g, V + 2).astype(i32)
         for v in range(V + 1):
             value = weight if v == V else weight * swapped(v)
-            for h in range(2):
-                for r in range(R):
-                    left[pl.ds(g * N * C + v * T + h * R + r, N, stride=C), :] = jnp.where(
-                        target == 2 * r + h, value, 0.0
-                    )
+            high[v, at] = value.astype(bf16).astype(f32)
+            low[v, at] = value - high[v, at]
 
     places = lax.broadcasted_iota(i32, (L, SLOTS), 0)
-
-    def scatter(s, carry):
-        at = pl.multiple_of(s * C, 8)
-        high, low = split(left[pl.ds(at, C), :])
-        hit = (places == column[pl.ds(s, 1), :]).astype(f32).astype(bf16)
+    parts = lax.broadcasted_iota(i32, (T, SLOTS), 0)
+    none = jnp.zeros((L, SLOTS), bf16)
+
+    def masked(values, s, part):
+        return jnp.concatenate([jnp.where(part, values[v, s : s + 1, :], 0.0) for v in range(V + 1)], axis=0)
+
+    for s in range(0, 2 * N, 2):
+        hits, values = [], []
+        for i in range(2):
+            target = place[s + i : s + i + 1, :]
+            hits.append((places == (target & (L - 1))).astype(f32).astype(bf16))
+            part = parts == ((target >> 8) + ((target >> 7) & 1) * R)
+            values.append(jnp.concatenate([masked(x, s + i, part) for x in (high, low)], axis=0).astype(bf16))
+        values = jnp.concatenate(values, axis=1)
+        hits = [jnp.concatenate([hits[0], none], axis=1), jnp.concatenate([none, hits[1]], axis=1)]
         spread = lax.dot_general(
-            jnp.concatenate([high, low], axis=0), hit, (((1,), (1,)), ((), ())), preferred_element_type=f32
+            values, jnp.concatenate(hits, axis=0), (((1,), (1,)), ((), ())), preferred_element_type=f32
         )
         spread = spread[:C] + spread[C:]
         keep = 1.0 - spread[Q:]
-        for v in range(V):
-            prep[pl.ds(at + v * T, T), :] = spread[v * T : (v + 1) * T] + keep * recv[pl.ds(at + v * T, T), :]
-        return carry
-
-    lax.fori_loop(0, 2 * N, scatter, 0, unroll=64)
+        for i in range(2):
+            cols = slice(i * L, (i + 1) * L)
+            for v in range(V):
+                at = slice((s + i) * C + v * T, (s + i) * C + (v + 1) * T)
+                prep[at, :] = spread[v * T : (v + 1) * T, cols] + keep[:, cols] * recv[at, :]
+
     for copy in fetch:
         copy.wait()
 
@@ -253,7 +261,8 @@
         out_specs=VMEM,
         scratch_shapes=[
             pltpu.VMEM((L * C, L), f32),
-            pltpu.VMEM((L * C, SLOTS), f32),
+            pltpu.VMEM((V + 1, L, SLOTS), f32),
+            pltpu.VMEM((V + 1, L, SLOTS), f32),
             pltpu.VMEM((L, SLOTS), i32),
             pltpu.VMEM((V * B, B), f32),
         ]

time: 175 us -> 174 us (level)
  no operation moved by 1% of the time
where the time goes in v1:
time: 174 us; the launch traced here: 173 us
  blocking collectives  70.2 us (40%)
  waiting for transfers between devices  67.1 us (39%)
  starting transfers between devices  16.7 us (10%)
  Pallas kernels  16.1 us (9%)
  local copies, waits for them, and re-layouts  2.85 us (2%)
    all_to_all x1, blocking collectives, exchange(): lax.all_to_all(value, ('half', 'slab'), split_axis=0, concat_axis=0, tile...  70.2 us
    ppermute x1, waiting for transfers between devices, local(): theirs = lax.ppermute(mine, 'half', [(0, 1), (1, 0)])  42.8 us
    all_to_all x1, waiting for transfers between devices, exchange(): lax.all_to_all(value, ('half', 'slab'), split_axis=0, concat_axis=0, tile...  24.3 us
    all_to_all x1, starting transfers between devices, exchange(): lax.all_to_all(value, ('half', 'slab'), split_axis=0, concat_axis=0, tile...  15 us
    pallas_call x1, Pallas kernels, planes(): pl.pallas_call(plane_kernel, out_shape=jax.ShapeDtypeStruct((L * Q, L), f...  8.56 us
    pallas_call x1, Pallas kernels, pack(): pl.pallas_call(pack_kernel, out_shape=jax.ShapeDtypeStruct((L, C, L), f32...  4.25 us
  transfers between devices with their start and end apart: 2, of which 2 were waited for; matrix products, arithmetic and copies ran while one was open for 0% of the time, Pallas kernels for 1%

profile of v1, /device:TPU:1, one launch (start us, length us, event | category | flops | bytes accessed | tf_op | source)
XLA Modules:
  0.0 173.2 jit_solution(15682912060095352590)
XLA Ops:
  0.0 4.3 %pack.1 = f32[128,48,128]{2,1,0:T(8,128)} custom-call(s32[2,64]{1,0:T(2,128)} %bitcast.30, s32[2,64]{1,0:T(2,128)} %bitcast.31, s32[1024]{0:T(1024)} %bitcast.28, s32[8,128]{1,0:T(8,128)} %bitcast.29, f32[5120,128]{1,0:T(8,128)} %bitcast.26, f32[1024,128]{1,0:T(8,128)} %bitcast.27), custom_call_target="tpu_custom_call" | custom-call | bytes 8000000 | tf_op jit(solution)/shard_map/pack/pallas_call | solution.py:214
  4.3 0.0 copy-start
  4.3 15.0 %all-to-all-start = ((f32[128,48,128]{2,1,0:T(8,128)}), f32[128,48,128]{2,1,0:T(8,128)S(1)}, u32[]{:S(2)}, u32[]{:S(2)}) async-start(f32[128,48,128]{2,1,0:T(8,128)} %pack.1), calls=%async_computation | async-start | bytes 6291456 | tf_op jit(solution)/shard_map/all_to_all | solution.py:291
  19.3 0.0 copy-done
  19.3 0.0 copy-start.1
  19.3 0.9 copy-done.1
  20.3 0.0 copy-start.2
  20.3 0.9 copy-done.2
  21.2 0.0 copy-start.3
  21.2 0.9 copy-done.3
  22.2 1.6 matrices.1.mine
  23.8 1.7 collective-permute-start
  25.5 42.8 %collective-permute-done.theirs = f32[4,256,256]{2,1,0:T(8,128)} collective-permute-done((f32[4,256,256]{2,1,0:T(8,128)}, f32[4,256,256]{2,1,0:T(8,128)}, u32[]{:S(2)}, u32[]{:S(2)}) %collective-permute-start) | collective-permute-done | bytes 1048608 | tf_op jit(solution)/shard_map/ppermute | solution.py:298
  68.2 24.3 %all-to-all-done = f32[128,48,128]{2,1,0:T(8,128)S(1)} async-done(((f32[128,48,128]{2,1,0:T(8,128)}), f32[128,48,128]{2,1,0:T(8,128)S(1)}, u32[]{:S(2)}, u32[]{:S(2)}) %all-to-all-start) | async-done | bytes 3145760 | tf_op jit(solution)/shard_map/all_to_all | solution.py:291
  92.5 8.6 %planes.1 = f32[5120,128]{1,0:T(8,128)S(1)} custom-call(s32[1]{0:T(128)} %bitcast.half, f32[6144,128]{1,0:T(8,128)S(1)} %bitcast.20, f32[4,256,256]{2,1,0:T(8,128)} %matrices.1.mine, f32[4,256,256]{2,1,0:T(8,128)} %collective-permute-done.theirs), custom_call_target="tpu_custom_call" | custom-call | flops 8000000000 | bytes 8000000 | tf_op jit(solution)/shard_map/planes/pallas_call | solution.py:257
  101.1 70.2 %all_to_all.10 = f32[128,40,128]{2,1,0:T(8,128)S(1)} all-to-all(f32[128,40,128]{2,1,0:T(8,128)S(1)} %bitcast.21), channel_id=1, replica_groups=mesh['pair'=2,'half'=2,'slab'=64] {'half','slab'}, dimensions={0} | all-to-all | bytes 5242880 | tf_op jit(solution)/shard_map/all_to_all | solution.py:291
  171.3 1.7 unpack.1
Async XLA Ops:
  4.3 15.0 %copy-start = (f32[1,256,256]{2,1,0:T(8,128)S(1)}, f32[1,256,256]{2,1,0:T(8,128)}, u32[]{:S(2)}) copy-start(f32[1,256,256]{2,1,0:T(8,128)} %param.14) | copy-start | bytes 786436
  4.3 88.2 %all-to-all-start = ((f32[128,48,128]{2,1,0:T(8,128)}), f32[128,48,128]{2,1,0:T(8,128)S(1)}, u32[]{:S(2)}, u32[]{:S(2)}) async-start(f32[128,48,128]{2,1,0:T(8,128)} %pack.1), calls=%async_computation | async-start | bytes 6291456 | tf_op jit(solution)/shard_map/all_to_all | solution.py:291
  19.3 1.0 copy-start.1
  20.3 0.9 copy-start.2
  21.2 0.9 copy-start.3
  23.8 44.5 %collective-permute-start = (f32[4,256,256]{2,1,0:T(8,128)}, f32[4,256,256]{2,1,0:T(8,128)}, u32[]{:S(2)}, u32[]{:S(2)}) collective-permute-start(f32[4,256,256]{2,1,0:T(8,128)} %matrices.1.mine), channel_id=1, source_target_pairs={{0,64},{64,0},{1,65},{65,1},{2,66},{66,2},{3,67},{67,3},{4,68},{68... | collective-permute-start | bytes 3145736 | tf_op jit(solution)/shard_map/ppermute | solution.py:298

commit v2 on v1

--- a/solution.py
+++ b/solution.py
@@ -15,6 +15,7 @@
 C = (V + 1) * T
 Q = V * T
 SLOTS = 128
+LEAD = 49
 NOWHERE = 4 * R * B
 EXTRA = Q
 FREE = (1.0, 0.5, 0.0, 0.0, 2.5)
@@ -136,7 +137,7 @@
     def masked(values, s, part):
         return jnp.concatenate([jnp.where(part, values[v, s : s + 1, :], 0.0) for v in range(V + 1)], axis=0)
 
-    for s in range(0, 2 * N, 2):
+    def scatter(s):
         hits, values = [], []
         for i in range(2):
             target = place[s + i : s + i + 1, :]
@@ -156,18 +157,10 @@
                 at = slice((s + i) * C + v * T, (s + i) * C + (v + 1) * T)
                 prep[at, :] = spread[v * T : (v + 1) * T, cols] + keep[:, cols] * recv[at, :]
 
-    for copy in fetch:
-        copy.wait()
-
-    for own in range(2):
-        grid = jnp.bitwise_xor(half[0], own)
-        da_h, da_l = split(here[own, 0])
-        db_h, db_l = split(here[own, 1])
-        fa_h, fa_l = split(here[own, 2])
-        fb_h, fb_l = split(here[own, 3])
+    def fluxes(g):
         for r in range(R):
             for h in range(2):
-                u = [prep[pl.ds(grid * (N * C) + v * T + h * R + r, N, stride=C), :] for v in range(V)]
+                u = [prep[pl.ds(g * N * C + v * T + h * R + r, N, stride=C), :] for v in range(V)]
                 cols = slice(h * L, (h + 1) * L)
                 inverse = 1.0 / u[0]
                 va, vb = u[1] * inverse, u[2] * inverse
@@ -176,26 +169,55 @@
                 flux_a = [u[1], u[1] * va + pressure, u[2] * va, u[3] * va, total * va]
                 flux_b = [u[2], u[1] * vb, u[2] * vb + pressure, u[3] * vb, total * vb]
                 for v in range(V):
-                    at = slice(v * B + r * N, v * B + (r + 1) * N)
+                    at = slice((g * V + v) * B + r * N, (g * V + v) * B + (r + 1) * N)
                     field[at, cols] = u[v]
                     ah[at, cols], al[at, cols] = split(flux_a[v])
                     bh[at, cols], bl[at, cols] = split(flux_b[v])
 
-        planes_at = [slice(v * B, (v + 1) * B) for v in range(V)]
-        for at in planes_at:
+    def products(g):
+        own = jnp.bitwise_xor(half[0], g)
+        (da_h, da_l), (db_h, db_l), (fa_h, fa_l), (fb_h, fb_l) = [split(here[own, m]) for m in range(4)]
+
+        def section(v, at):
             slope = dot(da_h, ah[at]) + dot(da_h, al[at]) + dot(da_l, ah[at])
             slope += dot(bh[at], db_h) + dot(bl[at], db_h) + dot(bh[at], db_l)
             ah[at], al[at] = split(field[at] - section_weight * slope)
-        for at in planes_at:
+
+        def second(v, at):
             smooth = dot(ah[at], fb_h) + dot(al[at], fb_h) + dot(ah[at], fb_l)
             bh[at], bl[at] = split(smooth)
-        for v, at in enumerate(planes_at):
+
+        def first(v, at):
             smooth = dot(fa_h, bh[at]) + dot(fa_h, bl[at]) + dot(fa_l, bh[at])
             for r in range(R):
                 for h in range(2):
-                    out[pl.ds(grid * (N * Q) + v * T + h * R + r, N, stride=Q), :] = smooth[
+                    out[pl.ds(g * N * Q + v * T + h * R + r, N, stride=Q), :] = smooth[
                         r * N : (r + 1) * N, h * L : (h + 1) * L
                     ]
+
+        return [
+            (lambda stage=stage, v=v: stage(v, slice((g * V + v) * B, (g * V + v + 1) * B)))
+            for stage in (section, second, first)
+            for v in range(V)
+        ]
+
+    pairs = list(range(0, 2 * N, 2))
+    later = pairs[LEAD:]
+    for s in pairs[:LEAD]:
+        scatter(s)
+    for copy in fetch:
+        copy.wait()
+    fluxes(0)
+    for step in products(0):
+        for s in later[:1]:
+            scatter(s)
+        later = later[1:]
+        step()
+    for s in later:
+        scatter(s)
+    fluxes(1)
+    for step in products(1):
+        step()
 
 
 def unpack_kernel(lines, result, out, sems):
@@ -264,9 +286,9 @@
             pltpu.VMEM((V + 1, L, SLOTS), f32),
             pltpu.VMEM((V + 1, L, SLOTS), f32),
             pltpu.VMEM((L, SLOTS), i32),
-            pltpu.VMEM((V * B, B), f32),
+            pltpu.VMEM((2 * V * B, B), f32),
         ]
-        + [pltpu.VMEM((V * B, B), bf16)] * 4
+        + [pltpu.VMEM((2 * V * B, B), bf16)] * 4
         + [pltpu.VMEM((2, 4, B, B), f32), pltpu.SemaphoreType.DMA((2,))],
         compiler_params=params(40),
         cost_estimate=cost(8_000_000, 8_000_000_000),

time: 174 us -> 173 us (level)
  no operation moved by 1% of the time
where the time goes in v2:
time: 173 us; the launch traced here: 172 us
  blocking collectives  70 us (40%)
  waiting for transfers between devices  67.1 us (39%)
  starting transfers between devices  16.7 us (10%)
  Pallas kernels  15.7 us (9%)
  local copies, waits for them, and re-layouts  2.85 us (2%)
    all_to_all x1, blocking collectives, exchange(): lax.all_to_all(value, ('half', 'slab'), split_axis=0, concat_axis=0, tile...  70 us
    ppermute x1, waiting for transfers between devices, local(): theirs = lax.ppermute(mine, 'half', [(0, 1), (1, 0)])  42.8 us
    all_to_all x1, waiting for transfers between devices, exchange(): lax.all_to_all(value, ('half', 'slab'), split_axis=0, concat_axis=0, tile...  24.3 us
    all_to_all x1, starting transfers between devices, exchange(): lax.all_to_all(value, ('half', 'slab'), split_axis=0, concat_axis=0, tile...  15 us
    pallas_call x1, Pallas kernels, planes(): pl.pallas_call(plane_kernel, out_shape=jax.ShapeDtypeStruct((L * Q, L), f...  8.07 us
    pallas_call x1, Pallas kernels, pack(): pl.pallas_call(pack_kernel, out_shape=jax.ShapeDtypeStruct((L, C, L), f32...  4.25 us
  transfers between devices with their start and end apart: 2, of which 2 were waited for; matrix products, arithmetic and copies ran while one was open for 0% of the time, Pallas kernels for 1%

profile of v2, /device:TPU:1, one launch (start us, length us, event | category | flops | bytes accessed | tf_op | source)
XLA Modules:
  0.0 172.4 jit_solution(18038780931571839050)
XLA Ops:
  0.0 4.3 %pack.1 = f32[128,48,128]{2,1,0:T(8,128)} custom-call(s32[2,64]{1,0:T(2,128)} %bitcast.30, s32[2,64]{1,0:T(2,128)} %bitcast.31, s32[1024]{0:T(1024)} %bitcast.28, s32[8,128]{1,0:T(8,128)} %bitcast.29, f32[5120,128]{1,0:T(8,128)} %bitcast.26, f32[1024,128]{1,0:T(8,128)} %bitcast.27), custom_call_target="tpu_custom_call" | custom-call | bytes 8000000 | tf_op jit(solution)/shard_map/pack/pallas_call | solution.py:236
  4.3 0.0 copy-start
  4.3 15.0 %all-to-all-start = ((f32[128,48,128]{2,1,0:T(8,128)}), f32[128,48,128]{2,1,0:T(8,128)S(1)}, u32[]{:S(2)}, u32[]{:S(2)}) async-start(f32[128,48,128]{2,1,0:T(8,128)} %pack.1), calls=%async_computation | async-start | bytes 6291456 | tf_op jit(solution)/shard_map/all_to_all | solution.py:313
  19.3 0.0 copy-done
  19.3 0.0 copy-start.1
  19.3 0.9 copy-done.1
  20.3 0.0 copy-start.2
  20.3 0.9 copy-done.2
  21.2 0.0 copy-start.3
  21.2 0.9 copy-done.3
  22.2 1.6 matrices.1.mine
  23.8 1.7 collective-permute-start
  25.5 42.8 %collective-permute-done.theirs = f32[4,256,256]{2,1,0:T(8,128)} collective-permute-done((f32[4,256,256]{2,1,0:T(8,128)}, f32[4,256,256]{2,1,0:T(8,128)}, u32[]{:S(2)}, u32[]{:S(2)}) %collective-permute-start) | collective-permute-done | bytes 1048608 | tf_op jit(solution)/shard_map/ppermute | solution.py:320
  68.2 24.3 %all-to-all-done = f32[128,48,128]{2,1,0:T(8,128)S(1)} async-done(((f32[128,48,128]{2,1,0:T(8,128)}), f32[128,48,128]{2,1,0:T(8,128)S(1)}, u32[]{:S(2)}, u32[]{:S(2)}) %all-to-all-start) | async-done | bytes 3145760 | tf_op jit(solution)/shard_map/all_to_all | solution.py:313
  92.5 8.1 %planes.1 = f32[5120,128]{1,0:T(8,128)S(1)} custom-call(s32[1]{0:T(128)} %bitcast.half, f32[6144,128]{1,0:T(8,128)S(1)} %bitcast.20, f32[4,256,256]{2,1,0:T(8,128)} %matrices.1.mine, f32[4,256,256]{2,1,0:T(8,128)} %collective-permute-done.theirs), custom_call_target="tpu_custom_call" | custom-call | flops 8000000000 | bytes 8000000 | tf_op jit(solution)/shard_map/planes/pallas_call | solution.py:279
  100.6 70.0 %all_to_all.10 = f32[128,40,128]{2,1,0:T(8,128)S(1)} all-to-all(f32[128,40,128]{2,1,0:T(8,128)S(1)} %bitcast.21), channel_id=1, replica_groups=mesh['pair'=2,'half'=2,'slab'=64] {'half','slab'}, dimensions={0} | all-to-all | bytes 5242880 | tf_op jit(solution)/shard_map/all_to_all | solution.py:313
  170.6 1.7 %unpack.1 = f32[5,4,256,128]{3,2,1,0:T(8,128)} custom-call(f32[5120,128]{1,0:T(8,128)S(1)} %bitcast.19), custom_call_target="tpu_custom_call" | custom-call | bytes 6000000 | tf_op jit(solution)/shard_map/unpack/pallas_call | solution.py:300
Async XLA Ops:
  4.3 15.0 %copy-start = (f32[1,256,256]{2,1,0:T(8,128)S(1)}, f32[1,256,256]{2,1,0:T(8,128)}, u32[]{:S(2)}) copy-start(f32[1,256,256]{2,1,0:T(8,128)} %param.14) | copy-start | bytes 786436
  4.3 88.2 %all-to-all-start = ((f32[128,48,128]{2,1,0:T(8,128)}), f32[128,48,128]{2,1,0:T(8,128)S(1)}, u32[]{:S(2)}, u32[]{:S(2)}) async-start(f32[128,48,128]{2,1,0:T(8,128)} %pack.1), calls=%async_computation | async-start | bytes 6291456 | tf_op jit(solution)/shard_map/all_to_all | solution.py:313
  19.3 1.0 copy-start.1
  20.3 0.9 copy-start.2
  21.2 0.9 copy-start.3
  23.8 44.5 %collective-permute-start = (f32[4,256,256]{2,1,0:T(8,128)}, f32[4,256,256]{2,1,0:T(8,128)}, u32[]{:S(2)}, u32[]{:S(2)}) collective-permute-start(f32[4,256,256]{2,1,0:T(8,128)} %matrices.1.mine), channel_id=1, source_target_pairs={{0,64},{64,0},{1,65},{65,1},{2,66},{66,2},{3,67},{67,3},{4,68},{68... | collective-permute-start | bytes 3145736 | tf_op jit(solution)/shard_map/ppermute | solution.py:320

commit v3 on v2

--- a/solution.py
+++ b/solution.py
@@ -15,7 +15,8 @@
 C = (V + 1) * T
 Q = V * T
 SLOTS = 128
-LEAD = 49
+LEAD = 34
+AHEAD = 2
 NOWHERE = 4 * R * B
 EXTRA = Q
 FREE = (1.0, 0.5, 0.0, 0.0, 2.5)
@@ -110,8 +111,11 @@
 
 def plane_kernel(half, recv, mine, theirs, out, prep, high, low, place, field, ah, al, bh, bl, here, sems):
     fetch = [pltpu.make_async_copy(mine, here.at[0], sems.at[0]), pltpu.make_async_copy(theirs, here.at[1], sems.at[1])]
-    for copy in fetch:
-        copy.start()
+    for own in range(2):
+        @pl.when(half[0] == own)
+        def _(own=own):
+            fetch[own].start()
+            fetch[1 - own].start()
 
     for g in range(2):
         def rows(grid, e):
@@ -201,21 +205,25 @@
             for v in range(V)
         ]
 
+    def arrived(g):
+        own = jnp.bitwise_xor(half[0], g)
+        pltpu.make_async_copy(mine, here.at[own], sems.at[own]).wait()
+
     pairs = list(range(0, 2 * N, 2))
     later = pairs[LEAD:]
     for s in pairs[:LEAD]:
         scatter(s)
-    for copy in fetch:
-        copy.wait()
+    arrived(0)
     fluxes(0)
     for step in products(0):
-        for s in later[:1]:
+        for s in later[:AHEAD]:
             scatter(s)
-        later = later[1:]
+        later = later[AHEAD:]
         step()
     for s in later:
         scatter(s)
     fluxes(1)
+    arrived(1)
     for step in products(1):
         step()
 

time: 173 us -> 173 us (level)
  no operation moved by 1% of the time
where the time goes in v3:
time: 173 us
  blocking collectives  70.2 us (41%)
  waiting for transfers between devices  67.1 us (39%)
  starting transfers between devices  16.7 us (10%)
  Pallas kernels  16.1 us (9%)
  local copies, waits for them, and re-layouts  2.85 us (2%)
    all_to_all x1, blocking collectives, exchange(): lax.all_to_all(value, ('half', 'slab'), split_axis=0, concat_axis=0, tile...  70.2 us
    ppermute x1, waiting for transfers between devices, local(): theirs = lax.ppermute(mine, 'half', [(0, 1), (1, 0)])  42.8 us
    all_to_all x1, waiting for transfers between devices, exchange(): lax.all_to_all(value, ('half', 'slab'), split_axis=0, concat_axis=0, tile...  24.3 us
    all_to_all x1, starting transfers between devices, exchange(): lax.all_to_all(value, ('half', 'slab'), split_axis=0, concat_axis=0, tile...  15 us
    pallas_call x1, Pallas kernels, planes(): pl.pallas_call(plane_kernel, out_shape=jax.ShapeDtypeStruct((L * Q, L), f...  8.51 us
    pallas_call x1, Pallas kernels, pack(): pl.pallas_call(pack_kernel, out_shape=jax.ShapeDtypeStruct((L, C, L), f32...  4.25 us
  transfers between devices with their start and end apart: 2, of which 2 were waited for; matrix products, arithmetic and copies ran while one was open for 0% of the time, Pallas kernels for 1%

profile of v3, /device:TPU:1, one launch (start us, length us, event | category | flops | bytes accessed | tf_op | source)
XLA Modules:
  0.0 173.1 jit_solution(18127840807641367192)
XLA Ops:
  0.0 4.3 %pack.1 = f32[128,48,128]{2,1,0:T(8,128)} custom-call(s32[2,64]{1,0:T(2,128)} %bitcast.30, s32[2,64]{1,0:T(2,128)} %bitcast.31, s32[1024]{0:T(1024)} %bitcast.28, s32[8,128]{1,0:T(8,128)} %bitcast.29, f32[5120,128]{1,0:T(8,128)} %bitcast.26, f32[1024,128]{1,0:T(8,128)} %bitcast.27), custom_call_target="tpu_custom_call" | custom-call | bytes 8000000 | tf_op jit(solution)/shard_map/pack/pallas_call | solution.py:244
  4.3 0.0 copy-start
  4.3 15.0 %all-to-all-start = ((f32[128,48,128]{2,1,0:T(8,128)}), f32[128,48,128]{2,1,0:T(8,128)S(1)}, u32[]{:S(2)}, u32[]{:S(2)}) async-start(f32[128,48,128]{2,1,0:T(8,128)} %pack.1), calls=%async_computation | async-start | bytes 6291456 | tf_op jit(solution)/shard_map/all_to_all | solution.py:321
  19.3 0.0 copy-done
  19.3 0.0 copy-start.1
  19.3 0.9 copy-done.1
  20.3 0.0 copy-start.2
  20.3 0.9 copy-done.2
  21.2 0.0 copy-start.3
  21.2 0.9 copy-done.3
  22.2 1.6 matrices.1.mine
  23.8 1.7 collective-permute-start
  25.5 42.8 %collective-permute-done.theirs = f32[4,256,256]{2,1,0:T(8,128)} collective-permute-done((f32[4,256,256]{2,1,0:T(8,128)}, f32[4,256,256]{2,1,0:T(8,128)}, u32[]{:S(2)}, u32[]{:S(2)}) %collective-permute-start) | collective-permute-done | bytes 1048608 | tf_op jit(solution)/shard_map/ppermute | solution.py:328
  68.2 24.3 %all-to-all-done = f32[128,48,128]{2,1,0:T(8,128)S(1)} async-done(((f32[128,48,128]{2,1,0:T(8,128)}), f32[128,48,128]{2,1,0:T(8,128)S(1)}, u32[]{:S(2)}, u32[]{:S(2)}) %all-to-all-start) | async-done | bytes 3145760 | tf_op jit(solution)/shard_map/all_to_all | solution.py:321
  92.5 8.5 %planes.1 = f32[5120,128]{1,0:T(8,128)S(1)} custom-call(s32[1]{0:T(128)} %bitcast.half, f32[6144,128]{1,0:T(8,128)S(1)} %bitcast.20, f32[4,256,256]{2,1,0:T(8,128)} %matrices.1.mine, f32[4,256,256]{2,1,0:T(8,128)} %collective-permute-done.theirs), custom_call_target="tpu_custom_call" | custom-call | flops 8000000000 | bytes 8000000 | tf_op jit(solution)/shard_map/planes/pallas_call | solution.py:287
  101.0 70.2 %all_to_all.10 = f32[128,40,128]{2,1,0:T(8,128)S(1)} all-to-all(f32[128,40,128]{2,1,0:T(8,128)S(1)} %bitcast.21), channel_id=1, replica_groups=mesh['pair'=2,'half'=2,'slab'=64] {'half','slab'}, dimensions={0} | all-to-all | bytes 5242880 | tf_op jit(solution)/shard_map/all_to_all | solution.py:321
  171.3 1.7 unpack.1
Async XLA Ops:
  4.3 15.0 %copy-start = (f32[1,256,256]{2,1,0:T(8,128)S(1)}, f32[1,256,256]{2,1,0:T(8,128)}, u32[]{:S(2)}) copy-start(f32[1,256,256]{2,1,0:T(8,128)} %param.14) | copy-start | bytes 786436
  4.3 88.2 %all-to-all-start = ((f32[128,48,128]{2,1,0:T(8,128)}), f32[128,48,128]{2,1,0:T(8,128)S(1)}, u32[]{:S(2)}, u32[]{:S(2)}) async-start(f32[128,48,128]{2,1,0:T(8,128)} %pack.1), calls=%async_computation | async-start | bytes 6291456 | tf_op jit(solution)/shard_map/all_to_all | solution.py:321
  19.3 1.0 copy-start.1
  20.3 0.9 copy-start.2
  21.2 0.9 copy-start.3
  23.8 44.5 %collective-permute-start = (f32[4,256,256]{2,1,0:T(8,128)}, f32[4,256,256]{2,1,0:T(8,128)}, u32[]{:S(2)}, u32[]{:S(2)}) collective-permute-start(f32[4,256,256]{2,1,0:T(8,128)} %matrices.1.mine), channel_id=1, source_target_pairs={{0,64},{64,0},{1,65},{65,1},{2,66},{66,2},{3,67},{67,3},{4,68},{68... | collective-permute-start | bytes 3145736 | tf_op jit(solution)/shard_map/ppermute | solution.py:328

commit v4 on v2

--- a/solution.py
+++ b/solution.py
@@ -15,7 +15,7 @@
 C = (V + 1) * T
 Q = V * T
 SLOTS = 128
-LEAD = 49
+LEAD = N
 NOWHERE = 4 * R * B
 EXTRA = Q
 FREE = (1.0, 0.5, 0.0, 0.0, 2.5)

time: 173 us -> 173 us (level)
  no operation moved by 1% of the time
where the time goes in v4:
time: 173 us
  blocking collectives  70.2 us (41%)
  waiting for transfers between devices  67.1 us (39%)
  starting transfers between devices  16.7 us (10%)
  Pallas kernels  16 us (9%)
  local copies, waits for them, and re-layouts  2.85 us (2%)
    all_to_all x1, blocking collectives, exchange(): lax.all_to_all(value, ('half', 'slab'), split_axis=0, concat_axis=0, tile...  70.2 us
    ppermute x1, waiting for transfers between devices, local(): theirs = lax.ppermute(mine, 'half', [(0, 1), (1, 0)])  42.8 us
    all_to_all x1, waiting for transfers between devices, exchange(): lax.all_to_all(value, ('half', 'slab'), split_axis=0, concat_axis=0, tile...  24.3 us
    all_to_all x1, starting transfers between devices, exchange(): lax.all_to_all(value, ('half', 'slab'), split_axis=0, concat_axis=0, tile...  15 us
    pallas_call x1, Pallas kernels, planes(): pl.pallas_call(plane_kernel, out_shape=jax.ShapeDtypeStruct((L * Q, L), f...  8.45 us
    pallas_call x1, Pallas kernels, pack(): pl.pallas_call(pack_kernel, out_shape=jax.ShapeDtypeStruct((L, C, L), f32...  4.25 us
  transfers between devices with their start and end apart: 2, of which 2 were waited for; matrix products, arithmetic and copies ran while one was open for 0% of the time, Pallas kernels for 1%

profile of v4, /device:TPU:1, one launch (start us, length us, event | category | flops | bytes accessed | tf_op | source)
XLA Modules:
  0.0 173.1 jit_solution(6464268358450832868)
XLA Ops:
  0.0 4.3 %pack.1 = f32[128,48,128]{2,1,0:T(8,128)} custom-call(s32[2,64]{1,0:T(2,128)} %bitcast.30, s32[2,64]{1,0:T(2,128)} %bitcast.31, s32[1024]{0:T(1024)} %bitcast.28, s32[8,128]{1,0:T(8,128)} %bitcast.29, f32[5120,128]{1,0:T(8,128)} %bitcast.26, f32[1024,128]{1,0:T(8,128)} %bitcast.27), custom_call_target="tpu_custom_call" | custom-call | bytes 8000000 | tf_op jit(solution)/shard_map/pack/pallas_call | solution.py:236
  4.3 0.0 copy-start
  4.3 15.0 %all-to-all-start = ((f32[128,48,128]{2,1,0:T(8,128)}), f32[128,48,128]{2,1,0:T(8,128)S(1)}, u32[]{:S(2)}, u32[]{:S(2)}) async-start(f32[128,48,128]{2,1,0:T(8,128)} %pack.1), calls=%async_computation | async-start | bytes 6291456 | tf_op jit(solution)/shard_map/all_to_all | solution.py:313
  19.3 0.0 copy-done
  19.3 0.0 copy-start.1
  19.3 0.9 copy-done.1
  20.3 0.0 copy-start.2
  20.3 0.9 copy-done.2
  21.2 0.0 copy-start.3
  21.2 0.9 copy-done.3
  22.2 1.6 matrices.1.mine
  23.8 1.7 collective-permute-start
  25.5 42.8 %collective-permute-done.theirs = f32[4,256,256]{2,1,0:T(8,128)} collective-permute-done((f32[4,256,256]{2,1,0:T(8,128)}, f32[4,256,256]{2,1,0:T(8,128)}, u32[]{:S(2)}, u32[]{:S(2)}) %collective-permute-start) | collective-permute-done | bytes 1048608 | tf_op jit(solution)/shard_map/ppermute | solution.py:320
  68.2 24.3 %all-to-all-done = f32[128,48,128]{2,1,0:T(8,128)S(1)} async-done(((f32[128,48,128]{2,1,0:T(8,128)}), f32[128,48,128]{2,1,0:T(8,128)S(1)}, u32[]{:S(2)}, u32[]{:S(2)}) %all-to-all-start) | async-done | bytes 3145760 | tf_op jit(solution)/shard_map/all_to_all | solution.py:313
  92.5 8.4 %planes.1 = f32[5120,128]{1,0:T(8,128)S(1)} custom-call(s32[1]{0:T(128)} %bitcast.half, f32[6144,128]{1,0:T(8,128)S(1)} %bitcast.20, f32[4,256,256]{2,1,0:T(8,128)} %matrices.1.mine, f32[4,256,256]{2,1,0:T(8,128)} %collective-permute-done.theirs), custom_call_target="tpu_custom_call" | custom-call | flops 8000000000 | bytes 8000000 | tf_op jit(solution)/shard_map/planes/pallas_call | solution.py:279
  101.0 70.2 %all_to_all.10 = f32[128,40,128]{2,1,0:T(8,128)S(1)} all-to-all(f32[128,40,128]{2,1,0:T(8,128)S(1)} %bitcast.21), channel_id=1, replica_groups=mesh['pair'=2,'half'=2,'slab'=64] {'half','slab'}, dimensions={0} | all-to-all | bytes 5242880 | tf_op jit(solution)/shard_map/all_to_all | solution.py:313
  171.2 1.7 unpack.1
Async XLA Ops:
  4.3 15.0 %copy-start = (f32[1,256,256]{2,1,0:T(8,128)S(1)}, f32[1,256,256]{2,1,0:T(8,128)}, u32[]{:S(2)}) copy-start(f32[1,256,256]{2,1,0:T(8,128)} %param.14) | copy-start | bytes 786436
  4.3 88.2 %all-to-all-start = ((f32[128,48,128]{2,1,0:T(8,128)}), f32[128,48,128]{2,1,0:T(8,128)S(1)}, u32[]{:S(2)}, u32[]{:S(2)}) async-start(f32[128,48,128]{2,1,0:T(8,128)} %pack.1), calls=%async_computation | async-start | bytes 6291456 | tf_op jit(solution)/shard_map/all_to_all | solution.py:313
  19.3 1.0 copy-start.1
  20.3 0.9 copy-start.2
  21.2 0.9 copy-start.3
  23.8 44.5 %collective-permute-start = (f32[4,256,256]{2,1,0:T(8,128)}, f32[4,256,256]{2,1,0:T(8,128)}, u32[]{:S(2)}, u32[]{:S(2)}) collective-permute-start(f32[4,256,256]{2,1,0:T(8,128)} %matrices.1.mine), channel_id=1, source_target_pairs={{0,64},{64,0},{1,65},{65,1},{2,66},{66,2},{3,67},{67,3},{4,68},{68... | collective-permute-start | bytes 3145736 | tf_op jit(solution)/shard_map/ppermute | solution.py:320
